TPU v7x, 32 devices: a whole 2x2x4 slice. The times are simulated.
32 devices in a mesh: row: 4 (over z), col: 8 (over y, x, core).
Axes of the slice: x: 2, y: 2, z: 4, core: 2. Of those that a mesh axis runs over, the one named last changes fastest.
Arguments:
- vertices: float32 [3, 3840], P(None, ('row', 'col')), may hold values from -6 to 6
- connect: int32 [4, 3840], P(None, ('row', 'col')), may hold values from 0 to 119
- component: int32 [3840], P(('row', 'col')), may hold values from 0 to 4
- azimuth: float32 [1], replicated, may hold values from 0 to 6.2831
- adjoint_rhs: float32 [24, 3840], P(None, ('row', 'col')), may hold values from -6 to 6
Outputs:
- solution: float32 [24, 3840], P(None, ('row', 'col'))
- residual_sq: float32 [24], replicated
Inputs may be any that keep to these rules, and one draw needn't show every extreme that they name: Entry connect[k, p] names vertex (p // 120) * 120 + connect[k, p], a vertex of the panel's own block. `component`: 0 marks a panel of the airframe body, b > 0 a panel of blade b.
All inputs are finite; a program needn't handle non-finite values.
Results may differ from a plain program's by a relative error of at most 0.0003.
Values sent between devices are 32-bit elements; how exact they have to be, the bound alone decides.
A program may use at most 64 MiB of HBM per device.

v0:
```python
import math

import jax
import jax.numpy as jnp
from jax import lax
from jax.sharding import PartitionSpec as P

BLADES = 4


epsilon = 1e-06
core_square = 0.04
highest = lax.Precision.HIGHEST


def panel_frame(corners, component, azimuth, blades):
    angle_turn = azimuth[0] + 2.0 * math.pi / blades * (component - 1).astype(jnp.float32)
    cosine = jnp.cos(angle_turn)[None, :]
    sine_turn = jnp.sin(angle_turn)[None, :]
    on_rotor = (component > 0)[None, :]
    xcoord = corners[0]
    ycoord = corners[1]
    turned_x = jnp.where(on_rotor, cosine * xcoord - sine_turn * ycoord, xcoord)
    turned_y = jnp.where(on_rotor, sine_turn * xcoord + cosine * ycoord, ycoord)
    placed = jnp.stack([turned_x, turned_y, corners[2]])
    centers = jnp.mean(placed, axis=1)
    diagonal_one = placed[:, 2] - placed[:, 0]
    diagonal_two = placed[:, 3] - placed[:, 1]
    areas = 0.5 * jnp.stack(
        [
            diagonal_one[1] * diagonal_two[2] - diagonal_one[2] * diagonal_two[1],
            diagonal_one[2] * diagonal_two[0] - diagonal_one[0] * diagonal_two[2],
            diagonal_one[0] * diagonal_two[1] - diagonal_one[1] * diagonal_two[0],
        ]
    )
    return jnp.concatenate([centers, areas], axis=0)


def influence(receivers, sources, scale):
    delta_x = receivers[0][:, None] - sources[0][None, :]
    delta_y = receivers[1][:, None] - sources[1][None, :]
    delta_z = receivers[2][:, None] - sources[2][None, :]
    inverse = lax.rsqrt(delta_x * delta_x + delta_y * delta_y + delta_z * delta_z + core_square)
    doublet = (
        sources[3][None, :] * delta_x
        + sources[4][None, :] * delta_y
        + sources[5][None, :] * delta_z
    ) * (inverse * inverse * inverse)
    return scale * (doublet + sources[5][None, :] * inverse)


def small_solve(start_norm, first_diag, first_sub, second_top, second_diag, second_sub):
    det_value = (
        second_sub * second_sub * (first_diag * first_diag + first_sub * first_sub)
        + (first_diag * second_diag - first_sub * second_top) ** 2
    )
    gram_00 = first_diag * first_diag + first_sub * first_sub
    gram_01 = first_diag * second_top + first_sub * second_diag
    gram_11 = second_top * second_top + second_diag * second_diag + second_sub * second_sub
    coef_one = start_norm * (gram_11 * first_diag - gram_01 * second_top) / det_value
    coef_two = start_norm * (gram_00 * second_top - gram_01 * first_diag) / det_value
    error_one = start_norm - first_diag * coef_one - second_top * coef_two
    error_two = -first_sub * coef_one - second_diag * coef_two
    error_three = -second_sub * coef_two
    return (
        coef_one,
        coef_two,
        error_one * error_one + error_two * error_two + error_three * error_three,
    )


def inner_sum(left, right):
    return jnp.sum(left * right, axis=1)


def on_device(vertices, connect, component, azimuth, adjoint_rhs):
    width = vertices.shape[1]
    order = width * lax.axis_size("row") * lax.axis_size("col")
    scale = 2.0 / math.sqrt(order)
    lookup = (connect[:, :, None] == jnp.arange(width, dtype=jnp.int32)[None, None, :]).astype(
        jnp.float32
    )
    corners = jnp.einsum("cv,kpv->ckp", vertices, lookup, precision=highest)
    frames = panel_frame(corners, component, azimuth, BLADES)
    diag_term = 3.0 + jnp.sqrt(jnp.sum(frames[3:] * frames[3:], axis=0))
    receiver_frames = lax.all_gather(frames, "col", axis=1, tiled=True)
    source_frames = lax.all_gather(frames, "row", axis=1, tiled=True)

    def apply_matrix(vector):
        partial_sums = jnp.dot(
            lax.all_gather(vector, "col", axis=1, tiled=True),
            influence(receiver_frames, source_frames, scale),
            precision=highest,
            preferred_element_type=jnp.float32,
        )
        summed = lax.psum_scatter(partial_sums, "row", scatter_dimension=1, tiled=True)
        return summed + diag_term[None, :] * vector

    start_norm = jnp.sqrt(lax.psum(inner_sum(adjoint_rhs, adjoint_rhs), ("row", "col")) + epsilon)
    basis_one = adjoint_rhs / start_norm[:, None]
    image_one = apply_matrix(basis_one)
    first_diag, image_square = lax.psum(
        (inner_sum(basis_one, image_one), inner_sum(image_one, image_one)), ("row", "col")
    )
    first_sub = jnp.sqrt(image_square - first_diag * first_diag + epsilon)
    basis_two = (image_one - first_diag[:, None] * basis_one) / first_sub[:, None]
    image_two = apply_matrix(basis_two)
    second_top, second_diag, second_square = lax.psum(
        (
            inner_sum(basis_one, image_two),
            inner_sum(basis_two, image_two),
            inner_sum(image_two, image_two),
        ),
        ("row", "col"),
    )
    second_sub = jnp.sqrt(
        second_square - second_top * second_top - second_diag * second_diag + epsilon
    )
    coef_one, coef_two, residual_sq = small_solve(
        start_norm, first_diag, first_sub, second_top, second_diag, second_sub
    )
    solution = coef_one[:, None] * basis_one + coef_two[:, None] * basis_two
    return (solution, residual_sq)


def solution(mesh):
    in_specs = (
        P(None, ("row", "col")),
        P(None, ("row", "col")),
        P(("row", "col")),
        P(),
        P(None, ("row", "col")),
    )
    out_specs = (P(None, ("row", "col")), P())
    return jax.shard_map(
        on_device, mesh=mesh, in_specs=in_specs, out_specs=out_specs, check_vma=False
    )
```

profile of v0, /device:TPU:0, one launch (start us, length us, event | category | flops | bytes accessed | tf_op | source)
XLA Modules:
  0.0 208.8 jit_solution(7759055734900084843)
XLA Ops:
  0.6 0.0 copy-start
  1.3 1.2 dynamic-slice
  2.5 0.0 copy-start.1
  3.2 0.7 broadcast_compare_fusion
  3.9 0.8 multiply_reduce_fusion.5
  4.7 42.0 %psum.42 = f32[24]{0:T(128)S(1)} all-reduce(f32[24]{0:T(128)S(1)} %multiply_reduce_fusion.5), channel_id=1, replica_groups=mesh['row'=4,'col'=8] {'row','col'}, use_global_device_ids=true, to_apply=%region_1.2 | all-reduce | flops 24 | bytes 192 | tf_op jit(solution)/shard_map/psum | solution.py:99
  46.7 0.7 fusion.20
  47.4 0.0 copy-done
  47.4 1.0 convolution_bitcast_fusion
  48.6 0.0 copy-done.1
  48.6 0.1 fusion.22
  48.7 13.1 %all-gather.1 = f32[4,120,6]{1,2,0:T(8,128)S(1)} all-gather(f32[1,120,6]{1,2,0:T(8,128)S(1)} %maximum_bitcast_fusion), channel_id=1, replica_groups=mesh['row'=4,'col'=8] {'row'}, dimensions={0}, use_global_device_ids=true | all-gather | bytes 14400 | tf_op jit(solution)/shard_map/all_gather | solution.py:87
  61.8 0.1 reshape.73
  61.9 9.8 %all-gather.2 = f32[8,120,6]{1,2,0:T(8,128)S(1)} all-gather(f32[1,120,6]{1,2,0:T(8,128)S(1)} %maximum_bitcast_fusion), channel_id=1, replica_groups=mesh['row'=4,'col'=8] {'col'}, dimensions={0}, use_global_device_ids=true | all-gather | bytes 25920 | tf_op jit(solution)/shard_map/all_gather | solution.py:86
  71.8 0.1 reshape.75
  71.9 8.3 %all-gather = f32[8,120,24]{1,2,0:T(8,128)S(1)} all-gather(f32[1,120,24]{1,2,0:T(8,128)S(1)} %fusion.22), channel_id=1, replica_groups=mesh['row'=4,'col'=8] {'col'}, dimensions={0}, use_global_device_ids=true | all-gather | bytes 103680 | tf_op jit(solution)/shard_map/all_gather | solution.py:91
  80.2 0.1 reshape.71
  80.3 2.5 %fusion.11 = f32[24,480]{1,0:T(8,128)S(1)} fusion(f32[960,24]{0,1:T(8,128)S(1)} %reshape.71, f32[480]{0:T(512)S(1)} %bitcast.61, f32[960]{0:T(1024)S(1)} %bitcast.55, f32[480]{0:T(512)S(1)} %bitcast.63, f32[480]{0:T(512)S(1)} %bitcast.65, f32[960]{0:T(1024)S(1)} %bitcast.57, f32[480]{0:T(512)S(1)} %bitcast.67, f32[480]{0:T(512)S(1)} %bitcast.69, ...), kind=kOutput, calls=%fused_computation.18 | convolution fusion | flops 141926400 | bytes 161280 | tf_op jit(solution)/shard_map/dot_general | solution.py:90
  82.7 18.2 %all-reduce = f32[24,480]{1,0:T(8,128)S(1)} all-reduce(f32[24,480]{1,0:T(8,128)S(1)} %fusion.11), channel_id=2, replica_groups=mesh['row'=4,'col'=8] {'row'}, use_global_device_ids=true, to_apply=%region_3.4.clone | all-reduce | flops 11520 | bytes 92160
  101.0 0.2 multiply_reduce_fusion.4
  101.2 37.5 %all-reduce.3 = (f32[24]{0:T(128)S(1)}, f32[24]{0:T(128)S(1)}) all-reduce(f32[24]{0:T(128)S(1)} %get-tuple-element.3, f32[24]{0:T(128)S(1)} %get-tuple-element.2), channel_id=1, replica_groups=mesh['row'=4,'col'=8] {'row','col'}, use_global_device_ids=true, to_apply=%region_8.9 | all-reduce | flops 48 | bytes 384 | tf_op jit(solution)/shard_map/psum | solution.py:102
  138.7 0.1 subtract_divide_fusion
  138.8 10.0 %all-gather.3 = f32[8,120,24]{1,2,0:T(8,128)S(1)} all-gather(f32[1,120,24]{1,2,0:T(8,128)S(1)} %bitcast.50), channel_id=1, replica_groups=mesh['row'=4,'col'=8] {'col'}, dimensions={0}, use_global_device_ids=true | all-gather | bytes 103680 | tf_op jit(solution)/shard_map/all_gather | solution.py:91
  148.8 0.1 reshape.77
  148.9 2.5 %fusion.9 = f32[24,480]{1,0:T(8,128)S(1)} fusion(f32[960,24]{0,1:T(8,128)S(1)} %reshape.77, f32[480]{0:T(512)S(1)} %bitcast.62, f32[960]{0:T(1024)S(1)} %bitcast.56, f32[480]{0:T(512)S(1)} %bitcast.64, f32[480]{0:T(512)S(1)} %bitcast.66, f32[960]{0:T(1024)S(1)} %bitcast.58, f32[480]{0:T(512)S(1)} %bitcast.68, f32[480]{0:T(512)S(1)} %bitcast.70, ...), kind=kOutput, calls=%fused_computation.17 | convolution fusion | flops 141926400 | bytes 161280 | tf_op jit(solution)/shard_map/dot_general | solution.py:90
  151.4 18.4 %all-reduce.1 = f32[24,480]{1,0:T(8,128)S(1)} all-reduce(f32[24,480]{1,0:T(8,128)S(1)} %fusion.9), channel_id=3, replica_groups=mesh['row'=4,'col'=8] {'row'}, use_global_device_ids=true, to_apply=%region_9.10.clone | all-reduce | flops 11520 | bytes 92160
  169.8 0.2 multiply_reduce_fusion
  170.0 37.6 %all-reduce.2 = (f32[24]{0:T(128)S(1)}, f32[24]{0:T(128)S(1)}, f32[24]{0:T(128)S(1)}) all-reduce(f32[24]{0:T(128)S(1)} %get-tuple-element.6, f32[24]{0:T(128)S(1)} %get-tuple-element.5, f32[24]{0:T(128)S(1)} %get-tuple-element.4), channel_id=1, replica_groups=mesh['row'=4,'col'=8] {'row','col'}, use_global_device_ids=true, to_apply=%region_11.12 | all-reduce | flops 72 | bytes 576 | tf_op jit(solution)/shard_map/psum | solution.py:108
  207.6 0.5 multiply_add_fusion.1
  208.1 0.7 multiply_add_fusion
  (15 shorter events, 0.2 us)
Async XLA Ops:
  0.6 46.8 %copy-start = (f32[3,120]{1,0:T(4,128)S(1)}, f32[3,120]{1,0:T(4,128)}, u32[]{:S(2)}) copy-start(f32[3,120]{1,0:T(4,128)} %param.5) | copy-start | bytes 4324
  2.5 46.1 %copy-start.1 = (f32[24,120]{1,0:T(8,128)S(1)}, f32[24,120]{1,0:T(8,128)}, u32[]{:S(2)}) copy-start(f32[24,120]{1,0:T(8,128)} %param.9) | copy-start | bytes 34564
where the time goes:
time: 210 us; the launch traced here: 209 us
  blocking collectives  195 us (93%)
  matrix products  6.03 us (3%)
  other arithmetic  4.12 us (2%)
    psum x1, blocking collectives, on_device(): lax.psum(inner_sum(adjoint_rhs, adjoint_rhs), ('row', 'col')) + epsilon  42 us
    psum x1, blocking collectives, on_device(): lax.psum((inner_sum(basis_one, image_two), inner_sum(basis_two, image_two...  37.6 us
    psum x1, blocking collectives, on_device(): lax.psum((inner_sum(basis_one, image_one), inner_sum(image_one, image_one...  37.5 us
    unnamed x2, blocking collectives  36.6 us
    all_gather x2, blocking collectives, apply_matrix(): lax.all_gather(vector, 'col', axis=1, tiled=True)  18.3 us
    all_gather x1, blocking collectives, on_device(): source_frames = lax.all_gather(frames, 'row', axis=1, tiled=True)  13.1 us
    all_gather x1, blocking collectives, on_device(): receiver_frames = lax.all_gather(frames, 'col', axis=1, tiled=True)  9.83 us
    dot_general x2, matrix products, apply_matrix(): jnp.dot(lax.all_gather(vector, 'col', axis=1, tiled=True), influence(rece...  4.99 us

commit v1 on v0

v1 whole, which is shorter than its diff:
```python
import functools
import math

import jax
import jax.numpy as jnp
from jax import lax
from jax.experimental import pallas as pl
from jax.experimental.pallas import tpu as pltpu
from jax.sharding import PartitionSpec as P

BLADES = 4
LANES = 128
SUB = 32

epsilon = 1e-06
core_square = 0.04
shift = 3.0


def panel_frame(corners, component, azimuth, blades):
    angle_turn = azimuth + 2.0 * math.pi / blades * (component - 1).astype(jnp.float32)
    cosine = jnp.cos(angle_turn)
    sine = jnp.sin(angle_turn)
    on_rotor = component > 0
    placed = []
    for corner in corners:
        x, y, z = corner[0:1], corner[1:2], corner[2:3]
        placed.append(
            (
                jnp.where(on_rotor, cosine * x - sine * y, x),
                jnp.where(on_rotor, sine * x + cosine * y, y),
                z,
            )
        )
    center = [
        (placed[0][k] + placed[1][k] + placed[2][k] + placed[3][k]) * 0.25 for k in range(3)
    ]
    one = [placed[2][k] - placed[0][k] for k in range(3)]
    two = [placed[3][k] - placed[1][k] for k in range(3)]
    area = [
        0.5 * (one[1] * two[2] - one[2] * two[1]),
        0.5 * (one[2] * two[0] - one[0] * two[2]),
        0.5 * (one[0] * two[1] - one[1] * two[0]),
    ]
    return center, area


def small_solve(gg, p1, p2, q0, q1, q2):
    n2 = gg + epsilon
    start_norm = jnp.sqrt(n2)
    one_one = gg / n2
    first_diag = p1 / n2 + shift * one_one
    sigma = (p1 - shift * epsilon) / n2
    uu = jnp.maximum((p2 - 2.0 * sigma * p1 + sigma * sigma * gg) / n2, 0.0)
    sub2 = uu + epsilon
    first_sub = jnp.sqrt(sub2)
    one_two = (p1 + shift * gg) * (epsilon / n2) / (n2 * first_sub)
    t0 = (q0 - sigma * p1) / (n2 * first_sub)
    second_top = t0 + shift * one_two
    two_two = uu / sub2
    t1 = (q1 - sigma * (p2 + q0 - sigma * p1)) / (n2 * sub2)
    second_diag = t1 + shift * two_two
    tau = t1 - shift * epsilon / sub2
    yy = (q2 - sigma * (2.0 * q1 - sigma * p2)) / (n2 * sub2)
    vv = (
        yy
        - 2.0 * (second_top * t0 + tau * t1)
        + second_top * second_top * one_one
        + tau * tau * two_two
        + 2.0 * second_top * tau * one_two
    )
    second_sub = jnp.sqrt(jnp.maximum(vv, 0.0) + epsilon)
    gram_00 = first_diag * first_diag + first_sub * first_sub
    cross = first_diag * second_diag - first_sub * second_top
    det_value = second_sub * second_sub * gram_00 + cross * cross
    gram_01 = first_diag * second_top + first_sub * second_diag
    gram_11 = second_top * second_top + second_diag * second_diag + second_sub * second_sub
    coef_one = start_norm * (gram_11 * first_diag - gram_01 * second_top) / det_value
    coef_two = start_norm * (gram_00 * second_top - gram_01 * first_diag) / det_value
    error_one = start_norm - first_diag * coef_one - second_top * coef_two
    error_two = -first_sub * coef_one - second_diag * coef_two
    error_three = -second_sub * coef_two
    residual = error_one * error_one + error_two * error_two + error_three * error_three
    of_w1 = coef_two / (start_norm * first_sub)
    of_g = coef_one / start_norm - sigma * of_w1
    return of_g, of_w1, residual


def split(value):
    twice = jnp.concatenate([value, value], axis=0)
    lead = twice.astype(jnp.bfloat16).astype(jnp.float32)
    row = lax.broadcasted_iota(jnp.int32, twice.shape, 0)
    return jnp.where(row < value.shape[0], lead, twice - lead).astype(jnp.bfloat16)


def kernel(
    nr, nc, width, rhs,
    azimuth_ref, vertices_ref, connect_ref, component_ref, rhs_ref,
    solution_ref, residual_ref,
    pad_f, pad_i, frames_col, frames_row, vec_col, image_col, halves, matrix,
    send_one, recv_one, send_two, recv_two, total_col, total_row,
    sems_fc, sems_fr, sems_g, sems_w, sems_one, sems_two, sems_tc, sems_tr,
):
    my_r, my_c = lax.axis_index("row"), lax.axis_index("col")
    scale = 2.0 / math.sqrt(width * nr * nc)
    cols = [lax.rem(my_c + k, nc) for k in range(1, nc)]
    rows = [lax.rem(my_r + k, nr) for k in range(1, nr)]

    barrier = pltpu.get_barrier_semaphore()
    for c in cols:
        pl.semaphore_signal(
            barrier, inc=1, device_id=(my_r, c), device_id_type=pl.DeviceIdType.MESH
        )
    for r in rows:
        pl.semaphore_signal(
            barrier, inc=1, device_id=(r, my_c), device_id_type=pl.DeviceIdType.MESH
        )

    started = []

    def push(source, target, sems, at_send, at_recv, device):
        copy = pltpu.make_async_remote_copy(
            src_ref=source,
            dst_ref=target,
            send_sem=sems.at[0, at_send],
            recv_sem=sems.at[1, at_recv],
            device_id=device,
            device_id_type=pl.DeviceIdType.MESH,
        )
        copy.start()
        started.append(copy)

    def to_plane(ref, sems):
        for c in cols:
            push(ref.at[my_c], ref.at[my_c], sems, c, my_c, (my_r, c))

    def to_line(source, ref, sems):
        for r in rows:
            at = my_r if source is None else r
            push((ref if source is None else source).at[at], ref.at[my_r], sems, r, my_r, (r, my_c))

    def arrived(ref, sems, at):
        pltpu.make_async_remote_copy(
            src_ref=ref.at[at],
            dst_ref=ref.at[at],
            send_sem=sems.at[0, at],
            recv_sem=sems.at[1, at],
            device_id=(my_r, my_c),
            device_id_type=pl.DeviceIdType.MESH,
        ).wait_recv()

    pad_f[...] = jnp.zeros_like(pad_f)
    pad_i[...] = jnp.zeros_like(pad_i)
    pad_f[0:3, 0:width] = vertices_ref[...]
    pad_i[0:4, 0:width] = connect_ref[...]
    pad_i[4:5, 0:width] = component_ref[...]
    vec_col[my_c] = jnp.zeros((rhs, LANES), jnp.float32)
    vec_col[my_c, :, 0:width] = rhs_ref[...]
    vertices = pad_f[...]
    corners = [
        jnp.take_along_axis(
            vertices,
            jnp.broadcast_to(pad_i[k : k + 1, :], vertices.shape),
            axis=1,
            mode="promise_in_bounds",
        )
        for k in range(4)
    ]
    center, area = panel_frame(corners, pad_i[4:5, :], azimuth_ref[0], BLADES)
    size = jnp.sqrt(area[0] * area[0] + area[1] * area[1] + area[2] * area[2])
    frame = jnp.concatenate(
        center + [scale * part for part in area] + [jnp.zeros((2, LANES), jnp.float32)], axis=0
    )
    frames_col[my_c] = frame
    frames_row[my_r] = frame

    pl.semaphore_wait(barrier, nc - 1 + nr - 1)
    to_line(None, frames_row, sems_fr)
    to_plane(frames_col, sems_fc)
    to_plane(vec_col, sems_g)

    def fill(c):
        columns = frames_col[c].T
        for s in range(LANES // SUB):
            x, y, z = (
                jnp.broadcast_to(columns[s * SUB : (s + 1) * SUB, k : k + 1], (SUB, LANES))
                for k in range(3)
            )
            place = pl.ds(pl.multiple_of(c * LANES + s * SUB, SUB), SUB)

            def one(r, carry):
                source = frames_row[r]
                dx, dy, dz = x - source[0:1], y - source[1:2], z - source[2:3]
                inverse = lax.rsqrt(dx * dx + dy * dy + (dz * dz + core_square))
                along = source[3:4] * dx + source[4:5] * dy + source[5:6] * dz
                value = inverse * (along * (inverse * inverse) + source[5:6])
                lead = value.astype(jnp.bfloat16)
                where = pl.ds(r * LANES if isinstance(r, int) else pl.multiple_of(r * LANES, LANES), LANES)
                matrix[0, place, where] = lead
                matrix[1, place, where] = (value - lead.astype(jnp.float32)).astype(jnp.bfloat16)
                return carry

            if nr <= 4:
                for r in range(nr):
                    one(r, 0)
            else:
                lax.fori_loop(0, nr, one, 0)

    def fill_step(k, carry):
        c = lax.rem(my_c + k, nc)
        arrived(frames_col, sems_fc, c)
        fill(c)
        return carry

    for r in rows:
        arrived(frames_row, sems_fr, r)
    fill(my_c)
    lax.fori_loop(1, nc, fill_step, 0)

    def place_halves(ref, c):
        halves[:, pl.ds(pl.multiple_of(c * LANES, LANES), LANES)] = split(ref[c])

    deep = min(nc, 8) * LANES

    def product(send, recv):
        def part(k):
            at = pl.ds(k * deep if isinstance(k, int) else pl.multiple_of(k * deep, deep), deep)
            return jnp.dot(
                halves[:, at], matrix[0, at, :], preferred_element_type=jnp.float32
            ) + jnp.dot(halves[:, at], matrix[1, at, :], preferred_element_type=jnp.float32)

        total = part(0)
        if nc * LANES > deep:
            total = lax.fori_loop(1, nc * LANES // deep, lambda k, t: t + part(k), total)
        total = total[:rhs] + total[rhs:]
        for r in range(nr):
            send[r] = total[:, r * LANES : (r + 1) * LANES]

    def apply_matrix(ref, send, recv, sems):
        product(send, recv)
        to_line(send, recv, sems)
        summed = send[my_r] + size * ref[my_c]
        for r in rows:
            arrived(recv, sems, r)
            summed = summed + recv[r]
        return summed

    place_halves(vec_col, my_c)
    for c in cols:
        arrived(vec_col, sems_g, c)
        place_halves(vec_col, c)
    w1 = apply_matrix(vec_col, send_one, recv_one, sems_one)
    image_col[my_c] = w1
    to_plane(image_col, sems_w)
    g = vec_col[my_c]
    lane = lax.broadcasted_iota(jnp.int32, (rhs, LANES), 1)

    def with_sum(tile, at, product):
        return jnp.where(lane == at, jnp.sum(product, axis=1, keepdims=True), tile)

    tile = jnp.zeros((rhs, LANES), jnp.float32)
    tile = with_sum(tile, 0, g * g)
    tile = with_sum(tile, 1, g * w1)
    tile = with_sum(tile, 2, w1 * w1)
    place_halves(image_col, my_c)
    for c in cols:
        arrived(image_col, sems_w, c)
        place_halves(image_col, c)
    w2 = apply_matrix(image_col, send_two, recv_two, sems_two)
    tile = with_sum(tile, 3, g * w2)
    tile = with_sum(tile, 4, w1 * w2)
    tile = with_sum(tile, 5, w2 * w2)

    total_col[my_c] = jnp.zeros((8, LANES), jnp.float32)
    total_col[my_c, :, 0:rhs] = tile.T[0:8, :]
    to_plane(total_col, sems_tc)
    for c in cols:
        arrived(total_col, sems_tc, c)
    total = total_col[0]
    for c in range(1, nc):
        total = total + total_col[c]
    total_row[my_r] = total
    to_line(None, total_row, sems_tr)
    for r in rows:
        arrived(total_row, sems_tr, r)
    total = total_row[0]
    for r in range(1, nr):
        total = total + total_row[r]
    of_g, of_w1, residual = small_solve(*(total[k : k + 1] for k in range(6)))
    residual_ref[...] = residual[:, 0:rhs]
    factors = jnp.concatenate([of_g, of_w1, jnp.zeros((6, LANES), jnp.float32)], axis=0).T
    answer = factors[0:rhs, 0:1] * g + factors[0:rhs, 1:2] * w1
    solution_ref[...] = answer[:, 0:width]
    for copy in started:
        copy.wait_send()


def on_device(nr, nc, vertices, connect, component, azimuth, adjoint_rhs):
    rhs, width = adjoint_rhs.shape
    vmem = pl.BlockSpec(memory_space=pltpu.VMEM)
    f32 = jnp.float32
    matrix_bytes = 2 * nc * nr * LANES * LANES * 2
    pair = lambda n: pltpu.SemaphoreType.DMA((2, n))
    answer, residual = pl.pallas_call(
        functools.partial(kernel, nr, nc, width, rhs),
        out_shape=(
            jax.ShapeDtypeStruct((rhs, width), f32),
            jax.ShapeDtypeStruct((1, rhs), f32),
        ),
        in_specs=[pl.BlockSpec(memory_space=pltpu.SMEM)] + [vmem] * 4,
        out_specs=(vmem, vmem),
        scratch_shapes=[
            pltpu.VMEM((8, LANES), f32),
            pltpu.VMEM((8, LANES), jnp.int32),
            pltpu.VMEM((nc, 8, LANES), f32),
            pltpu.VMEM((nr, 8, LANES), f32),
            pltpu.VMEM((nc, rhs, LANES), f32),
            pltpu.VMEM((nc, rhs, LANES), f32),
            pltpu.VMEM((2 * rhs, nc * LANES), jnp.bfloat16),
            pltpu.VMEM((2, nc * LANES, nr * LANES), jnp.bfloat16),
            pltpu.VMEM((nr, rhs, LANES), f32),
            pltpu.VMEM((nr, rhs, LANES), f32),
            pltpu.VMEM((nr, rhs, LANES), f32),
            pltpu.VMEM((nr, rhs, LANES), f32),
            pltpu.VMEM((nc, 8, LANES), f32),
            pltpu.VMEM((nr, 8, LANES), f32),
            pair(nc), pair(nr), pair(nc), pair(nc), pair(nr), pair(nr), pair(nc), pair(nr),
        ],
        compiler_params=pltpu.CompilerParams(
            collective_id=0,
            has_side_effects=True,
            vmem_limit_bytes=matrix_bytes + 20 * 1024 * 1024,
        ),
        cost_estimate=pl.CostEstimate(
            flops=2 * matrix_bytes * rhs, bytes_accessed=4 * rhs * width * 3, transcendentals=0
        ),
    )(azimuth, vertices, connect, component.reshape(1, width), adjoint_rhs)
    return answer, residual.reshape(rhs)


def solution(mesh):
    in_specs = (
        P(None, ("row", "col")),
        P(None, ("row", "col")),
        P(("row", "col")),
        P(),
        P(None, ("row", "col")),
    )
    out_specs = (P(None, ("row", "col")), P())
    return jax.shard_map(
        functools.partial(on_device, mesh.shape["row"], mesh.shape["col"]),
        mesh=mesh,
        in_specs=in_specs,
        out_specs=out_specs,
        check_vma=False,
    )
```

time: 210 us -> 36 us (0.17)
  blocking collectives: 195 us -> 0 us
  Pallas kernels: 0 us -> 31.3 us
  matrix products: 6.03 us -> 0 us
  other arithmetic: 4.12 us -> 0 us
    psum x3 -> x0, blocking collectives: 117 us -> none  [the longest x1 42 us: on_device(): lax.psum(inner_sum(adjoint_rhs, adjoint_rhs), ('row', 'col')) + epsilon]
    all_gather x4 -> x0, blocking collectives: 41.2 us -> none  [the longest x2 18.3 us: apply_matrix(): lax.all_gather(vector, 'col', axis=1, tiled=True)]
    unnamed x2 -> x0, blocking collectives: 36.6 us -> none
    pallas_call x0 -> x1, Pallas kernels: none -> 31.3 us  [on_device(): pl.pallas_call(functools.partial(kernel, nr, nc, width, rhs), out_shape=(...]
    dot_general x3 -> x0, matrix products: 6.03 us -> none  [the longest x2 4.99 us: apply_matrix(): jnp.dot(lax.all_gather(vector, 'col', axis=1, tiled=True), influence(rece...]
where the time goes in v1:
time: 36 us; the launch traced here: 35.8 us
  Pallas kernels  31.3 us (87%)
  local copies, waits for them, and re-layouts  3.15 us (9%)
  between operations  1.32 us (4%)
    pallas_call x1, Pallas kernels, on_device(): pl.pallas_call(functools.partial(kernel, nr, nc, width, rhs), out_shape=(...  31.3 us
    unnamed x10, local copies, waits for them, and re-layouts  3.15 us

profile of v1, /device:TPU:0, one launch (start us, length us, event | category | flops | bytes accessed | tf_op | source)
XLA Modules:
  0.0 35.8 jit_solution(5274444329509663197)
XLA Ops:
  0.6 0.0 copy-start.1
  1.3 0.0 copy-start.3
  1.3 0.0 copy-done.1
  1.3 0.6 %copy-done.3 = s32[120]{0:T(128)S(1)} copy-done((s32[120]{0:T(128)S(1)}, s32[120]{0:T(128)}, u32[]{:S(2)}) %copy-start.3) | copy-done | bytes 504
  2.0 0.0 copy-start
  2.0 0.7 %copy-done = f32[24,120]{1,0:T(8,128)S(1)} copy-done((f32[24,120]{1,0:T(8,128)S(1)}, f32[24,120]{1,0:T(8,128)}, u32[]{:S(2)}) %copy-start) | copy-done | bytes 11544
  2.7 0.0 copy-start.2
  2.7 0.7 %copy-done.2 = s32[4,120]{1,0:T(4,128)S(1)} copy-done((s32[4,120]{1,0:T(4,128)S(1)}, s32[4,120]{1,0:T(4,128)}, u32[]{:S(2)}) %copy-start.2) | copy-done | bytes 1944
  3.3 31.3 %shard_map.68 = (f32[24,120]{1,0:T(8,128)S(1)}, f32[1,24]{1,0:T(1,128)S(1)}) custom-call(f32[1]{0:T(128)S(6)} %copy.9.azimuth_ref, f32[3,120]{1,0:T(4,128)S(1)} %copy-done.1, s32[4,120]{1,0:T(4,128)S(1)} %copy-done.2, s32[1,120]{1,0:T(1,128)S(1)} %bitcast.2, f32[24,120]{1,0:T(8,128)S(1)} %copy-done), custom_call_target="tpu_custom_call" | custom-call | flops 100663296 | bytes 34560 | tf_op jit(solution)/shard_map/pallas_call | solution.py:304
  34.6 0.6 %copy.10 = f32[24,120]{1,0:T(8,128)} copy(f32[24,120]{1,0:T(8,128)S(1)} %get-tuple-element.8) | data formatting | bytes 23040
  35.2 0.5 %copy.11 = f32[24]{0:T(128)} copy(f32[24]{0:T(128)S(1)} %bitcast.3) | data formatting | bytes 192
Async XLA Ops:
  0.6 0.7 %copy-start.1 = (f32[3,120]{1,0:T(4,128)S(1)}, f32[3,120]{1,0:T(4,128)}, u32[]{:S(2)}) copy-start(f32[3,120]{1,0:T(4,128)} %vertices_ref.1) | copy-start | bytes 4324
  1.3 0.7 %copy-start.3 = (s32[120]{0:T(128)S(1)}, s32[120]{0:T(128)}, u32[]{:S(2)}) copy-start(s32[120]{0:T(128)} %param.7) | copy-start | bytes 1444
  2.0 0.7 %copy-start = (f32[24,120]{1,0:T(8,128)S(1)}, f32[24,120]{1,0:T(8,128)}, u32[]{:S(2)}) copy-start(f32[24,120]{1,0:T(8,128)} %rhs_ref.1) | copy-start | bytes 34564
  2.7 0.7 %copy-start.2 = (s32[4,120]{1,0:T(4,128)S(1)}, s32[4,120]{1,0:T(4,128)}, u32[]{:S(2)}) copy-start(s32[4,120]{1,0:T(4,128)} %connect_ref.1) | copy-start | bytes 5764

commit v2 on v1

--- a/solution.py
+++ b/solution.py
@@ -95,8 +95,9 @@
 
 def kernel(
     nr, nc, width, rhs,
-    azimuth_ref, vertices_ref, connect_ref, component_ref, rhs_ref,
+    azimuth_in, vertices_in, connect_in, component_in, rhs_in,
     solution_ref, residual_ref,
+    azimuth_ref, vertices_ref, connect_ref, component_ref, rhs_ref, sems_in,
     pad_f, pad_i, frames_col, frames_row, vec_col, image_col, halves, matrix,
     send_one, recv_one, send_two, recv_two, total_col, total_row,
     sems_fc, sems_fr, sems_g, sems_w, sems_one, sems_two, sems_tc, sems_tr,
@@ -106,6 +107,20 @@
     cols = [lax.rem(my_c + k, nc) for k in range(1, nc)]
     rows = [lax.rem(my_r + k, nr) for k in range(1, nr)]
 
+    loads = [
+        pltpu.make_async_copy(source, target, sems_in.at[k])
+        for k, (source, target) in enumerate(
+            (
+                (azimuth_in, azimuth_ref),
+                (vertices_in, vertices_ref),
+                (connect_in, connect_ref),
+                (component_in, component_ref),
+                (rhs_in, rhs_ref),
+            )
+        )
+    ]
+    for load in loads:
+        load.start()
     barrier = pltpu.get_barrier_semaphore()
     for c in cols:
         pl.semaphore_signal(
@@ -151,10 +166,12 @@
 
     pad_f[...] = jnp.zeros_like(pad_f)
     pad_i[...] = jnp.zeros_like(pad_i)
+    vec_col[my_c] = jnp.zeros((rhs, LANES), jnp.float32)
+    for load in loads:
+        load.wait()
     pad_f[0:3, 0:width] = vertices_ref[...]
     pad_i[0:4, 0:width] = connect_ref[...]
     pad_i[4:5, 0:width] = component_ref[...]
-    vec_col[my_c] = jnp.zeros((rhs, LANES), jnp.float32)
     vec_col[my_c, :, 0:width] = rhs_ref[...]
     vertices = pad_f[...]
     corners = [
@@ -220,24 +237,34 @@
     def place_halves(ref, c):
         halves[:, pl.ds(pl.multiple_of(c * LANES, LANES), LANES)] = split(ref[c])
 
-    deep = min(nc, 8) * LANES
-
-    def product(send, recv):
-        def part(k):
-            at = pl.ds(k * deep if isinstance(k, int) else pl.multiple_of(k * deep, deep), deep)
-            return jnp.dot(
+    def product(ref, sems):
+        def chip(k, total):
+            first = lax.rem(my_c // 2 + k, nc // 2) * 2
+            for c in (first, first + 1):
+
+                @pl.when(c != my_c)
+                def _():
+                    arrived(ref, sems, c)
+
+                place_halves(ref, c)
+            at = pl.ds(pl.multiple_of(first * LANES, 2 * LANES), 2 * LANES)
+            part = jnp.dot(
                 halves[:, at], matrix[0, at, :], preferred_element_type=jnp.float32
             ) + jnp.dot(halves[:, at], matrix[1, at, :], preferred_element_type=jnp.float32)
-
-        total = part(0)
-        if nc * LANES > deep:
-            total = lax.fori_loop(1, nc * LANES // deep, lambda k, t: t + part(k), total)
-        total = total[:rhs] + total[rhs:]
+            return part if total is None else total + part
+
+        total = chip(0, None)
+        if nc <= 8:
+            for k in range(1, nc // 2):
+                total = chip(k, total)
+        else:
+            total = lax.fori_loop(1, nc // 2, chip, total)
+        return total[:rhs] + total[rhs:]
+
+    def apply_matrix(ref, sems_ref, send, recv, sems):
+        total = product(ref, sems_ref)
         for r in range(nr):
             send[r] = total[:, r * LANES : (r + 1) * LANES]
-
-    def apply_matrix(ref, send, recv, sems):
-        product(send, recv)
         to_line(send, recv, sems)
         summed = send[my_r] + size * ref[my_c]
         for r in rows:
@@ -245,11 +272,7 @@
             summed = summed + recv[r]
         return summed
 
-    place_halves(vec_col, my_c)
-    for c in cols:
-        arrived(vec_col, sems_g, c)
-        place_halves(vec_col, c)
-    w1 = apply_matrix(vec_col, send_one, recv_one, sems_one)
+    w1 = apply_matrix(vec_col, sems_g, send_one, recv_one, sems_one)
     image_col[my_c] = w1
     to_plane(image_col, sems_w)
     g = vec_col[my_c]
@@ -262,11 +285,7 @@
     tile = with_sum(tile, 0, g * g)
     tile = with_sum(tile, 1, g * w1)
     tile = with_sum(tile, 2, w1 * w1)
-    place_halves(image_col, my_c)
-    for c in cols:
-        arrived(image_col, sems_w, c)
-        place_halves(image_col, c)
-    w2 = apply_matrix(image_col, send_two, recv_two, sems_two)
+    w2 = apply_matrix(image_col, sems_w, send_two, recv_two, sems_two)
     tile = with_sum(tile, 3, g * w2)
     tile = with_sum(tile, 4, w1 * w2)
     tile = with_sum(tile, 5, w2 * w2)
@@ -307,9 +326,15 @@
             jax.ShapeDtypeStruct((rhs, width), f32),
             jax.ShapeDtypeStruct((1, rhs), f32),
         ),
-        in_specs=[pl.BlockSpec(memory_space=pltpu.SMEM)] + [vmem] * 4,
+        in_specs=[pl.BlockSpec(memory_space=pltpu.HBM)] * 5,
         out_specs=(vmem, vmem),
         scratch_shapes=[
+            pltpu.SMEM((1,), f32),
+            pltpu.VMEM((3, width), f32),
+            pltpu.VMEM((4, width), jnp.int32),
+            pltpu.VMEM((1, width), jnp.int32),
+            pltpu.VMEM((rhs, width), f32),
+            pltpu.SemaphoreType.DMA((5,)),
             pltpu.VMEM((8, LANES), f32),
             pltpu.VMEM((8, LANES), jnp.int32),
             pltpu.VMEM((nc, 8, LANES), f32),
@@ -329,7 +354,7 @@
         compiler_params=pltpu.CompilerParams(
             collective_id=0,
             has_side_effects=True,
-            vmem_limit_bytes=matrix_bytes + 20 * 1024 * 1024,
+            vmem_limit_bytes=64 * 1024 * 1024,
         ),
         cost_estimate=pl.CostEstimate(
             flops=2 * matrix_bytes * rhs, bytes_accessed=4 * rhs * width * 3, transcendentals=0

time: 36 us -> 35.3 us (0.981)
  local copies, waits for them, and re-layouts: 3.15 us -> 1.82 us
  Pallas kernels: 31.3 us -> 31.9 us
    unnamed x10 -> x4, local copies, waits for them, and re-layouts: 3.15 us -> 1.82 us
    pallas_call x1, Pallas kernels: 31.3 us -> 31.9 us  [on_device(): pl.pallas_call(functools.partial(kernel, nr, nc, width, rhs), out_shape=(...]
where the time goes in v2:
time: 35.3 us; the launch traced here: 35.1 us
  Pallas kernels  31.9 us (90%)
  local copies, waits for them, and re-layouts  1.82 us (5%)
  between operations  1.29 us (4%)
    pallas_call x1, Pallas kernels, on_device(): pl.pallas_call(functools.partial(kernel, nr, nc, width, rhs), out_shape=(...  31.9 us
    unnamed x4, local copies, waits for them, and re-layouts  1.82 us

profile of v2, /device:TPU:0, one launch (start us, length us, event | category | flops | bytes accessed | tf_op | source)
XLA Modules:
  0.0 35.1 jit_solution(3233883504248756158)
XLA Ops:
  1.3 31.9 %shard_map.68 = (f32[24,120]{1,0:T(8,128)}, f32[1,24]{1,0:T(1,128)}) custom-call(f32[1]{0:T(128)S(6)} %copy.9.azimuth_in, f32[3,120]{1,0:T(4,128)} %vertices_in.1, s32[4,120]{1,0:T(4,128)} %connect_in.1, s32[1,120]{1,0:T(1,128)} %bitcast.2, f32[24,120]{1,0:T(8,128)} %rhs_in.1), custom_call_target="tpu_custom_call" | custom-call | flops 100663296 | bytes 34560 | tf_op jit(solution)/shard_map/pallas_call | solution.py:323
  33.2 0.0 copy-start
  33.2 1.3 %copy.10 = f32[24,120]{1,0:T(8,128)} copy(f32[24,120]{1,0:T(8,128)} %get-tuple-element.8) | data formatting | bytes 23040
  34.6 0.0 copy-done
  34.6 0.5 %copy.11 = f32[24]{0:T(128)} copy(f32[24]{0:T(128)S(1)} %bitcast.3) | data formatting | bytes 192
Async XLA Ops:
  33.2 1.3 %copy-start = (f32[1,24]{1,0:T(1,128)S(1)}, f32[1,24]{1,0:T(1,128)}, u32[]{:S(2)}) copy-start(f32[1,24]{1,0:T(1,128)} %get-tuple-element.5) | copy-start | bytes 292

commit v3 on v2

--- a/solution.py
+++ b/solution.py
@@ -99,8 +99,8 @@
     solution_ref, residual_ref,
     azimuth_ref, vertices_ref, connect_ref, component_ref, rhs_ref, sems_in,
     pad_f, pad_i, frames_col, frames_row, vec_col, image_col, halves, matrix,
-    send_one, recv_one, send_two, recv_two, total_col, total_row,
-    sems_fc, sems_fr, sems_g, sems_w, sems_one, sems_two, sems_tc, sems_tr,
+    send_one, recv_one, send_two, recv_two, total_row, total_all,
+    sems_fc, sems_fr, sems_g, sems_w, sems_one, sems_two, sems_tr, sems_ta,
 ):
     my_r, my_c = lax.axis_index("row"), lax.axis_index("col")
     scale = 2.0 / math.sqrt(width * nr * nc)
@@ -122,14 +122,30 @@
     for load in loads:
         load.start()
     barrier = pltpu.get_barrier_semaphore()
-    for c in cols:
+    devices = nr * nc
+    me = my_r * nc + my_c
+    order = sorted(range(1, devices), key=lambda k: abs(k - devices // 2))
+
+    def each_other(act):
+        def step(k, carry):
+            act(lax.rem(me + k, devices))
+            return carry
+
+        if devices <= 64:
+            for k in order:
+                step(k, 0)
+        else:
+            lax.fori_loop(1, devices, step, 0)
+
+    def greet(other):
         pl.semaphore_signal(
-            barrier, inc=1, device_id=(my_r, c), device_id_type=pl.DeviceIdType.MESH
-        )
-    for r in rows:
-        pl.semaphore_signal(
-            barrier, inc=1, device_id=(r, my_c), device_id_type=pl.DeviceIdType.MESH
-        )
+            barrier,
+            inc=1,
+            device_id=(other // nc, lax.rem(other, nc)),
+            device_id_type=pl.DeviceIdType.MESH,
+        )
+
+    each_other(greet)
 
     started = []
 
@@ -191,7 +207,7 @@
     frames_col[my_c] = frame
     frames_row[my_r] = frame
 
-    pl.semaphore_wait(barrier, nc - 1 + nr - 1)
+    pl.semaphore_wait(barrier, devices - 1)
     to_line(None, frames_row, sems_fr)
     to_plane(frames_col, sems_fc)
     to_plane(vec_col, sems_g)
@@ -261,11 +277,13 @@
             total = lax.fori_loop(1, nc // 2, chip, total)
         return total[:rhs] + total[rhs:]
 
-    def apply_matrix(ref, sems_ref, send, recv, sems):
+    def apply_matrix(ref, sems_ref, send, recv, sems, beside=None):
         total = product(ref, sems_ref)
         for r in range(nr):
             send[r] = total[:, r * LANES : (r + 1) * LANES]
         to_line(send, recv, sems)
+        if beside is not None:
+            beside()
         summed = send[my_r] + size * ref[my_c]
         for r in rows:
             arrived(recv, sems, r)
@@ -276,42 +294,74 @@
     image_col[my_c] = w1
     to_plane(image_col, sems_w)
     g = vec_col[my_c]
-    lane = lax.broadcasted_iota(jnp.int32, (rhs, LANES), 1)
-
-    def with_sum(tile, at, product):
-        return jnp.where(lane == at, jnp.sum(product, axis=1, keepdims=True), tile)
-
-    tile = jnp.zeros((rhs, LANES), jnp.float32)
-    tile = with_sum(tile, 0, g * g)
-    tile = with_sum(tile, 1, g * w1)
-    tile = with_sum(tile, 2, w1 * w1)
-    w2 = apply_matrix(image_col, sems_w, send_two, recv_two, sems_two)
-    tile = with_sum(tile, 3, g * w2)
-    tile = with_sum(tile, 4, w1 * w2)
-    tile = with_sum(tile, 5, w2 * w2)
-
-    total_col[my_c] = jnp.zeros((8, LANES), jnp.float32)
-    total_col[my_c, :, 0:rhs] = tile.T[0:8, :]
-    to_plane(total_col, sems_tc)
-    for c in cols:
-        arrived(total_col, sems_tc, c)
-    total = total_col[0]
-    for c in range(1, nc):
-        total = total + total_col[c]
-    total_row[my_r] = total
-    to_line(None, total_row, sems_tr)
+    stride = LANES // 4
+    across = lax.broadcasted_iota(jnp.int32, (rhs, LANES), 1) - lax.broadcasted_iota(
+        jnp.int32, (rhs, LANES), 0
+    )
+
+    def as_row(products):
+        tile = jnp.zeros((rhs, LANES), jnp.float32)
+        for k, values in enumerate(products):
+            tile = jnp.where(
+                across == k * stride, jnp.sum(values, axis=1, keepdims=True), tile
+            )
+        return jnp.sum(tile, axis=0, keepdims=True)
+
+    def fields(row):
+        return [row[:, k * stride : k * stride + rhs] for k in range(3)]
+
+    def plane_sums():
+        def add(c, sums):
+            u, v = vec_col[c], image_col[c]
+            return sums[0] + u * u, sums[1] + u * v, sums[2] + v * v
+
+        sums = (jnp.zeros((rhs, LANES), jnp.float32),) * 3
+        if nc <= 8:
+            for c in range(nc):
+                sums = add(c, sums)
+        else:
+            sums = lax.fori_loop(0, nc, add, sums)
+        total_row[my_r] = as_row(sums)
+        to_line(None, total_row, sems_tr)
+
+    w2 = apply_matrix(image_col, sems_w, send_two, recv_two, sems_two, plane_sums)
+
+    total_all[me] = as_row((g * w2, w1 * w2, w2 * w2))
+
+    def last(other):
+        return pltpu.make_async_remote_copy(
+            src_ref=total_all.at[me],
+            dst_ref=total_all.at[me],
+            send_sem=sems_ta.at[0, other],
+            recv_sem=sems_ta.at[1, me],
+            device_id=(other // nc, lax.rem(other, nc)),
+            device_id_type=pl.DeviceIdType.MESH,
+        )
+
+    each_other(lambda other: last(other).start())
     for r in rows:
         arrived(total_row, sems_tr, r)
-    total = total_row[0]
+    early = total_row[0]
     for r in range(1, nr):
-        total = total + total_row[r]
-    of_g, of_w1, residual = small_solve(*(total[k : k + 1] for k in range(6)))
-    residual_ref[...] = residual[:, 0:rhs]
-    factors = jnp.concatenate([of_g, of_w1, jnp.zeros((6, LANES), jnp.float32)], axis=0).T
+        early = early + total_row[r]
+    each_other(lambda other: arrived(total_all, sems_ta, other))
+    if devices <= 64:
+        parts = [total_all[k] for k in range(devices)]
+        while len(parts) > 1:
+            parts = [sum(parts[k : k + 2][1:], parts[k]) for k in range(0, len(parts), 2)]
+        late = parts[0]
+    else:
+        late = lax.fori_loop(1, devices, lambda k, t: t + total_all[k], total_all[0])
+    of_g, of_w1, residual = small_solve(*fields(early), *fields(late))
+    residual_ref[...] = residual
+    pad_f[0:1, 0:rhs] = of_g
+    pad_f[1:2, 0:rhs] = of_w1
+    factors = pad_f[...].T
     answer = factors[0:rhs, 0:1] * g + factors[0:rhs, 1:2] * w1
     solution_ref[...] = answer[:, 0:width]
     for copy in started:
         copy.wait_send()
+    each_other(lambda other: last(other).wait_send())
 
 
 def on_device(nr, nc, vertices, connect, component, azimuth, adjoint_rhs):
@@ -347,19 +397,19 @@
             pltpu.VMEM((nr, rhs, LANES), f32),
             pltpu.VMEM((nr, rhs, LANES), f32),
             pltpu.VMEM((nr, rhs, LANES), f32),
-            pltpu.VMEM((nc, 8, LANES), f32),
-            pltpu.VMEM((nr, 8, LANES), f32),
-            pair(nc), pair(nr), pair(nc), pair(nc), pair(nr), pair(nr), pair(nc), pair(nr),
+            pltpu.VMEM((nr, 1, LANES), f32),
+            pltpu.VMEM((nr * nc, 1, LANES), f32),
+            pair(nc), pair(nr), pair(nc), pair(nc), pair(nr), pair(nr), pair(nr), pair(nr * nc),
         ],
         compiler_params=pltpu.CompilerParams(
             collective_id=0,
             has_side_effects=True,
-            vmem_limit_bytes=64 * 1024 * 1024,
+            vmem_limit_bytes=matrix_bytes + 20 * 1024 * 1024,
         ),
         cost_estimate=pl.CostEstimate(
             flops=2 * matrix_bytes * rhs, bytes_accessed=4 * rhs * width * 3, transcendentals=0
         ),
-    )(azimuth, vertices, connect, component.reshape(1, width), adjoint_rhs)
+    )(azimuth, *(pltpu.with_memory_space_constraint(x, pltpu.HBM) for x in (vertices, connect, component.reshape(1, width), adjoint_rhs)))
     return answer, residual.reshape(rhs)
 
 

time: 35.3 us -> 35 us (level)
  local copies, waits for them, and re-layouts: 1.82 us -> 1.11 us
  Pallas kernels: 31.9 us -> 32.5 us
    unnamed x4 -> x2, local copies, waits for them, and re-layouts: 1.82 us -> 1.11 us
    pallas_call x1, Pallas kernels: 31.9 us -> 32.5 us  [on_device(): pl.pallas_call(functools.partial(kernel, nr, nc, width, rhs), out_shape=(...]
where the time goes in v3:
time: 35 us; the launch traced here: 34.9 us
  Pallas kernels  32.5 us (93%)
  between operations  1.29 us (4%)
  local copies, waits for them, and re-layouts  1.11 us (3%)
    pallas_call x1, Pallas kernels, on_device(): pl.pallas_call(functools.partial(kernel, nr, nc, width, rhs), out_shape=(...  32.5 us
    unnamed x2, local copies, waits for them, and re-layouts  1.11 us

profile of v3, /device:TPU:0, one launch (start us, length us, event | category | flops | bytes accessed | tf_op | source)
XLA Modules:
  0.0 34.9 jit_solution(8044813958353763853)
XLA Ops:
  1.3 32.5 %shard_map.68 = (f32[24,120]{1,0:T(8,128)S(1)}, f32[1,24]{1,0:T(1,128)S(1)}) custom-call(f32[1]{0:T(128)S(6)} %copy.9.azimuth_in, f32[3,120]{1,0:T(4,128)} %vertices_in.1, s32[4,120]{1,0:T(4,128)} %connect_in.1, s32[1,120]{1,0:T(1,128)} %bitcast.3, f32[24,120]{1,0:T(8,128)} %rhs_in.1), custom_call_target="tpu_custom_call" | custom-call | flops 100663296 | bytes 34560 | tf_op jit(solution)/shard_map/pallas_call | solution.py:373
  33.7 0.6 %copy.10 = f32[24,120]{1,0:T(8,128)} copy(f32[24,120]{1,0:T(8,128)S(1)} %get-tuple-element.8) | data formatting | bytes 23040
  34.3 0.5 %copy.11 = f32[24]{0:T(128)} copy(f32[24]{0:T(128)S(1)} %bitcast.2) | data formatting | bytes 192

commit v4 on v3

--- a/solution.py
+++ b/solution.py
@@ -99,13 +99,17 @@
     solution_ref, residual_ref,
     azimuth_ref, vertices_ref, connect_ref, component_ref, rhs_ref, sems_in,
     pad_f, pad_i, frames_col, frames_row, vec_col, image_col, halves, matrix,
-    send_one, recv_one, send_two, recv_two, total_row, total_all,
-    sems_fc, sems_fr, sems_g, sems_w, sems_one, sems_two, sems_tr, sems_ta,
+    send_one, recv_one, send_two, recv_two, total_row, total_col, total_end,
+    sems_fc, sems_fr, sems_g, sems_w, sems_one, sems_two, sems_tr, sems_tc, sems_te,
 ):
     my_r, my_c = lax.axis_index("row"), lax.axis_index("col")
     scale = 2.0 / math.sqrt(width * nr * nc)
-    cols = [lax.rem(my_c + k, nc) for k in range(1, nc)]
-    rows = [lax.rem(my_r + k, nr) for k in range(1, nr)]
+
+    def each_col(act):
+        lax.fori_loop(1, nc, lambda k, carry: (act(lax.rem(my_c + k, nc)), carry)[1], 0)
+
+    def each_row(act):
+        lax.fori_loop(1, nr, lambda k, carry: (act(lax.rem(my_r + k, nr)), carry)[1], 0)
 
     loads = [
         pltpu.make_async_copy(source, target, sems_in.at[k])
@@ -122,53 +126,37 @@
     for load in loads:
         load.start()
     barrier = pltpu.get_barrier_semaphore()
-    devices = nr * nc
-    me = my_r * nc + my_c
-    order = sorted(range(1, devices), key=lambda k: abs(k - devices // 2))
-
-    def each_other(act):
-        def step(k, carry):
-            act(lax.rem(me + k, devices))
-            return carry
-
-        if devices <= 64:
-            for k in order:
-                step(k, 0)
-        else:
-            lax.fori_loop(1, devices, step, 0)
-
-    def greet(other):
+
+    def greet(device):
         pl.semaphore_signal(
-            barrier,
-            inc=1,
-            device_id=(other // nc, lax.rem(other, nc)),
-            device_id_type=pl.DeviceIdType.MESH,
+            barrier, inc=1, device_id=device, device_id_type=pl.DeviceIdType.MESH
         )
 
-    each_other(greet)
+    each_col(lambda c: greet((my_r, c)))
+    each_row(lambda r: greet((r, my_c)))
 
     started = []
 
-    def push(source, target, sems, at_send, at_recv, device):
-        copy = pltpu.make_async_remote_copy(
-            src_ref=source,
-            dst_ref=target,
-            send_sem=sems.at[0, at_send],
-            recv_sem=sems.at[1, at_recv],
-            device_id=device,
-            device_id_type=pl.DeviceIdType.MESH,
-        )
-        copy.start()
-        started.append(copy)
+    def push(each, source, target, sems, at_recv, device):
+        def copy(other):
+            return pltpu.make_async_remote_copy(
+                src_ref=source(other),
+                dst_ref=target,
+                send_sem=sems.at[0, other],
+                recv_sem=sems.at[1, at_recv],
+                device_id=device(other),
+                device_id_type=pl.DeviceIdType.MESH,
+            )
+
+        each(lambda other: copy(other).start())
+        started.append((each, lambda other: copy(other).wait_send()))
 
     def to_plane(ref, sems):
-        for c in cols:
-            push(ref.at[my_c], ref.at[my_c], sems, c, my_c, (my_r, c))
+        push(each_col, lambda c: ref.at[my_c], ref.at[my_c], sems, my_c, lambda c: (my_r, c))
 
     def to_line(source, ref, sems):
-        for r in rows:
-            at = my_r if source is None else r
-            push((ref if source is None else source).at[at], ref.at[my_r], sems, r, my_r, (r, my_c))
+        pick = (lambda r: ref.at[my_r]) if source is None else (lambda r: source.at[r])
+        push(each_row, pick, ref.at[my_r], sems, my_r, lambda r: (r, my_c))
 
     def arrived(ref, sems, at):
         pltpu.make_async_remote_copy(
@@ -207,7 +195,7 @@
     frames_col[my_c] = frame
     frames_row[my_r] = frame
 
-    pl.semaphore_wait(barrier, devices - 1)
+    pl.semaphore_wait(barrier, nc - 1 + nr - 1)
     to_line(None, frames_row, sems_fr)
     to_plane(frames_col, sems_fc)
     to_plane(vec_col, sems_g)
@@ -241,14 +229,16 @@
 
     def fill_step(k, carry):
         c = lax.rem(my_c + k, nc)
-        arrived(frames_col, sems_fc, c)
+
+        @pl.when(k > 0)
+        def _():
+            arrived(frames_col, sems_fc, c)
+
         fill(c)
         return carry
 
-    for r in rows:
-        arrived(frames_row, sems_fr, r)
-    fill(my_c)
-    lax.fori_loop(1, nc, fill_step, 0)
+    each_row(lambda r: arrived(frames_row, sems_fr, r))
+    lax.fori_loop(0, nc, fill_step, 0)
 
     def place_halves(ref, c):
         halves[:, pl.ds(pl.multiple_of(c * LANES, LANES), LANES)] = split(ref[c])
@@ -267,14 +257,10 @@
             part = jnp.dot(
                 halves[:, at], matrix[0, at, :], preferred_element_type=jnp.float32
             ) + jnp.dot(halves[:, at], matrix[1, at, :], preferred_element_type=jnp.float32)
-            return part if total is None else total + part
-
-        total = chip(0, None)
-        if nc <= 8:
-            for k in range(1, nc // 2):
-                total = chip(k, total)
-        else:
-            total = lax.fori_loop(1, nc // 2, chip, total)
+            return total + part
+
+        total = jnp.zeros((2 * rhs, nr * LANES), jnp.float32)
+        total = lax.fori_loop(0, nc // 2, chip, total)
         return total[:rhs] + total[rhs:]
 
     def apply_matrix(ref, sems_ref, send, recv, sems, beside=None):
@@ -282,13 +268,11 @@
         for r in range(nr):
             send[r] = total[:, r * LANES : (r + 1) * LANES]
         to_line(send, recv, sems)
+        recv[my_r] = send[my_r]
         if beside is not None:
             beside()
-        summed = send[my_r] + size * ref[my_c]
-        for r in rows:
-            arrived(recv, sems, r)
-            summed = summed + recv[r]
-        return summed
+        each_row(lambda r: arrived(recv, sems, r))
+        return size * ref[my_c] + jnp.sum(recv[...], axis=0)
 
     w1 = apply_matrix(vec_col, sems_g, send_one, recv_one, sems_one)
     image_col[my_c] = w1
@@ -316,42 +300,20 @@
             return sums[0] + u * u, sums[1] + u * v, sums[2] + v * v
 
         sums = (jnp.zeros((rhs, LANES), jnp.float32),) * 3
-        if nc <= 8:
-            for c in range(nc):
-                sums = add(c, sums)
-        else:
-            sums = lax.fori_loop(0, nc, add, sums)
-        total_row[my_r] = as_row(sums)
+        total_row[my_r] = as_row(lax.fori_loop(0, nc, add, sums))
         to_line(None, total_row, sems_tr)
 
     w2 = apply_matrix(image_col, sems_w, send_two, recv_two, sems_two, plane_sums)
 
-    total_all[me] = as_row((g * w2, w1 * w2, w2 * w2))
-
-    def last(other):
-        return pltpu.make_async_remote_copy(
-            src_ref=total_all.at[me],
-            dst_ref=total_all.at[me],
-            send_sem=sems_ta.at[0, other],
-            recv_sem=sems_ta.at[1, me],
-            device_id=(other // nc, lax.rem(other, nc)),
-            device_id_type=pl.DeviceIdType.MESH,
-        )
-
-    each_other(lambda other: last(other).start())
-    for r in rows:
-        arrived(total_row, sems_tr, r)
-    early = total_row[0]
-    for r in range(1, nr):
-        early = early + total_row[r]
-    each_other(lambda other: arrived(total_all, sems_ta, other))
-    if devices <= 64:
-        parts = [total_all[k] for k in range(devices)]
-        while len(parts) > 1:
-            parts = [sum(parts[k : k + 2][1:], parts[k]) for k in range(0, len(parts), 2)]
-        late = parts[0]
-    else:
-        late = lax.fori_loop(1, devices, lambda k, t: t + total_all[k], total_all[0])
+    total_col[my_c] = as_row((g * w2, w1 * w2, w2 * w2))
+    to_plane(total_col, sems_tc)
+    each_row(lambda r: arrived(total_row, sems_tr, r))
+    early = jnp.sum(total_row[...], axis=0)
+    each_col(lambda c: arrived(total_col, sems_tc, c))
+    total_end[my_r] = jnp.sum(total_col[...], axis=0)
+    to_line(None, total_end, sems_te)
+    each_row(lambda r: arrived(total_end, sems_te, r))
+    late = jnp.sum(total_end[...], axis=0)
     of_g, of_w1, residual = small_solve(*fields(early), *fields(late))
     residual_ref[...] = residual
     pad_f[0:1, 0:rhs] = of_g
@@ -359,9 +321,8 @@
     factors = pad_f[...].T
     answer = factors[0:rhs, 0:1] * g + factors[0:rhs, 1:2] * w1
     solution_ref[...] = answer[:, 0:width]
-    for copy in started:
-        copy.wait_send()
-    each_other(lambda other: last(other).wait_send())
+    for each, finish in started:
+        each(finish)
 
 
 def on_device(nr, nc, vertices, connect, component, azimuth, adjoint_rhs):
@@ -398,8 +359,9 @@
             pltpu.VMEM((nr, rhs, LANES), f32),
             pltpu.VMEM((nr, rhs, LANES), f32),
             pltpu.VMEM((nr, 1, LANES), f32),
-            pltpu.VMEM((nr * nc, 1, LANES), f32),
-            pair(nc), pair(nr), pair(nc), pair(nc), pair(nr), pair(nr), pair(nr), pair(nr * nc),
+            pltpu.VMEM((nc, 1, LANES), f32),
+            pltpu.VMEM((nr, 1, LANES), f32),
+            pair(nc), pair(nr), pair(nc), pair(nc), pair(nr), pair(nr), pair(nr), pair(nc), pair(nr),
         ],
         compiler_params=pltpu.CompilerParams(
             collective_id=0,

time: 35 us -> 35.4 us (1.011)
    pallas_call x1, Pallas kernels: 32.5 us -> 32.8 us  [on_device(): pl.pallas_call(functools.partial(kernel, nr, nc, width, rhs), out_shape=(...]
where the time goes in v4:
time: 35.4 us; the launch traced here: 35.2 us
  Pallas kernels  32.8 us (93%)
  between operations  1.29 us (4%)
  local copies, waits for them, and re-layouts  1.11 us (3%)
    pallas_call x1, Pallas kernels, on_device(): pl.pallas_call(functools.partial(kernel, nr, nc, width, rhs), out_shape=(...  32.8 us
    unnamed x2, local copies, waits for them, and re-layouts  1.11 us

profile of v4, /device:TPU:0, one launch (start us, length us, event | category | flops | bytes accessed | tf_op | source)
XLA Modules:
  0.0 35.2 jit_solution(10291406269761529358)
XLA Ops:
  1.3 32.8 %shard_map.68 = (f32[24,120]{1,0:T(8,128)S(1)}, f32[1,24]{1,0:T(1,128)S(1)}) custom-call(f32[1]{0:T(128)S(6)} %copy.9.azimuth_in, f32[3,120]{1,0:T(4,128)} %vertices_in.1, s32[4,120]{1,0:T(4,128)} %connect_in.1, s32[1,120]{1,0:T(1,128)} %bitcast.3, f32[24,120]{1,0:T(8,128)} %rhs_in.1), custom_call_target="tpu_custom_call" | custom-call | flops 100663296 | bytes 34560 | tf_op jit(solution)/shard_map/pallas_call | solution.py:334
  34.1 0.6 %copy.10 = f32[24,120]{1,0:T(8,128)} copy(f32[24,120]{1,0:T(8,128)S(1)} %get-tuple-element.8) | data formatting | bytes 23040
  34.7 0.5 %copy.11 = f32[24]{0:T(128)} copy(f32[24]{0:T(128)S(1)} %bitcast.2) | data formatting | bytes 192

commit v5 on v4

--- a/solution.py
+++ b/solution.py
@@ -105,11 +105,18 @@
     my_r, my_c = lax.axis_index("row"), lax.axis_index("col")
     scale = 2.0 / math.sqrt(width * nr * nc)
 
+    def loop(start, stop, step, carry):
+        if stop <= 8:
+            for k in range(start, stop):
+                carry = step(k, carry)
+            return carry
+        return lax.fori_loop(start, stop, step, carry)
+
     def each_col(act):
-        lax.fori_loop(1, nc, lambda k, carry: (act(lax.rem(my_c + k, nc)), carry)[1], 0)
+        loop(1, nc, lambda k, carry: (act(lax.rem(my_c + k, nc)), carry)[1], 0)
 
     def each_row(act):
-        lax.fori_loop(1, nr, lambda k, carry: (act(lax.rem(my_r + k, nr)), carry)[1], 0)
+        loop(1, nr, lambda k, carry: (act(lax.rem(my_r + k, nr)), carry)[1], 0)
 
     loads = [
         pltpu.make_async_copy(source, target, sems_in.at[k])
@@ -260,7 +267,7 @@
             return total + part
 
         total = jnp.zeros((2 * rhs, nr * LANES), jnp.float32)
-        total = lax.fori_loop(0, nc // 2, chip, total)
+        total = loop(0, nc // 2, chip, total)
         return total[:rhs] + total[rhs:]
 
     def apply_matrix(ref, sems_ref, send, recv, sems, beside=None):
@@ -300,7 +307,7 @@
             return sums[0] + u * u, sums[1] + u * v, sums[2] + v * v
 
         sums = (jnp.zeros((rhs, LANES), jnp.float32),) * 3
-        total_row[my_r] = as_row(lax.fori_loop(0, nc, add, sums))
+        total_row[my_r] = as_row(loop(0, nc, add, sums))
         to_line(None, total_row, sems_tr)
 
     w2 = apply_matrix(image_col, sems_w, send_two, recv_two, sems_two, plane_sums)

time: 35.4 us -> 34.5 us (0.975)
  Pallas kernels: 32.8 us -> 31.9 us
    pallas_call x1, Pallas kernels: 32.8 us -> 31.9 us  [on_device(): pl.pallas_call(functools.partial(kernel, nr, nc, width, rhs), out_shape=(...]
where the time goes in v5:
time: 34.5 us; the launch traced here: 34.3 us
  Pallas kernels  31.9 us (92%)
  between operations  1.29 us (4%)
  local copies, waits for them, and re-layouts  1.11 us (3%)
    pallas_call x1, Pallas kernels, on_device(): pl.pallas_call(functools.partial(kernel, nr, nc, width, rhs), out_shape=(...  31.9 us
    unnamed x2, local copies, waits for them, and re-layouts  1.11 us

profile of v5, /device:TPU:0, one launch (start us, length us, event | category | flops | bytes accessed | tf_op | source)
XLA Modules:
  0.0 34.3 jit_solution(6641581888899512617)
XLA Ops:
  1.3 31.9 %shard_map.68 = (f32[24,120]{1,0:T(8,128)S(1)}, f32[1,24]{1,0:T(1,128)S(1)}) custom-call(f32[1]{0:T(128)S(6)} %copy.9.azimuth_in, f32[3,120]{1,0:T(4,128)} %vertices_in.1, s32[4,120]{1,0:T(4,128)} %connect_in.1, s32[1,120]{1,0:T(1,128)} %bitcast.3, f32[24,120]{1,0:T(8,128)} %rhs_in.1), custom_call_target="tpu_custom_call" | custom-call | flops 100663296 | bytes 34560 | tf_op jit(solution)/shard_map/pallas_call | solution.py:341
  33.2 0.6 %copy.10 = f32[24,120]{1,0:T(8,128)} copy(f32[24,120]{1,0:T(8,128)S(1)} %get-tuple-element.8) | data formatting | bytes 23040
  33.8 0.5 %copy.11 = f32[24]{0:T(128)} copy(f32[24]{0:T(128)S(1)} %bitcast.2) | data formatting | bytes 192

commit v6 on v5

--- a/solution.py
+++ b/solution.py
@@ -207,14 +207,21 @@
     to_plane(frames_col, sems_fc)
     to_plane(vec_col, sems_g)
 
-    def fill(c):
+    def at_slot(k, step, offset, length):
+        start = k * step + offset
+        return pl.ds(start if isinstance(start, int) else pl.multiple_of(start, SUB), length)
+
+    def block_at(k):
+        return lax.rem(my_c // 2 + k // 2, nc // 2) * 2 + k % 2
+
+    def fill(k, c):
         columns = frames_col[c].T
         for s in range(LANES // SUB):
             x, y, z = (
                 jnp.broadcast_to(columns[s * SUB : (s + 1) * SUB, k : k + 1], (SUB, LANES))
                 for k in range(3)
             )
-            place = pl.ds(pl.multiple_of(c * LANES + s * SUB, SUB), SUB)
+            place = at_slot(k, LANES, s * SUB, SUB)
 
             def one(r, carry):
                 source = frames_row[r]
@@ -235,32 +242,33 @@
                 lax.fori_loop(0, nr, one, 0)
 
     def fill_step(k, carry):
-        c = lax.rem(my_c + k, nc)
-
-        @pl.when(k > 0)
+        c = block_at(k)
+
+        @pl.when(c != my_c)
         def _():
             arrived(frames_col, sems_fc, c)
 
-        fill(c)
+        fill(k, c)
         return carry
 
     each_row(lambda r: arrived(frames_row, sems_fr, r))
-    lax.fori_loop(0, nc, fill_step, 0)
-
-    def place_halves(ref, c):
-        halves[:, pl.ds(pl.multiple_of(c * LANES, LANES), LANES)] = split(ref[c])
+    loop(0, nc, fill_step, 0)
+
+    def lane_slot(k, length):
+        start = k * LANES
+        return pl.ds(start if isinstance(start, int) else pl.multiple_of(start, LANES), length)
 
     def product(ref, sems):
         def chip(k, total):
-            first = lax.rem(my_c // 2 + k, nc // 2) * 2
-            for c in (first, first + 1):
+            for j in (0, 1):
+                c = block_at(2 * k + j)
 
                 @pl.when(c != my_c)
                 def _():
                     arrived(ref, sems, c)
 
-                place_halves(ref, c)
-            at = pl.ds(pl.multiple_of(first * LANES, 2 * LANES), 2 * LANES)
+                halves[:, lane_slot(2 * k + j, LANES)] = split(ref[c])
+            at = lane_slot(2 * k, 2 * LANES)
             part = jnp.dot(
                 halves[:, at], matrix[0, at, :], preferred_element_type=jnp.float32
             ) + jnp.dot(halves[:, at], matrix[1, at, :], preferred_element_type=jnp.float32)

time: 34.5 us -> 34.5 us (level)
  no operation moved by 1% of the time
where the time goes in v6:
time: 34.5 us; the launch traced here: 34.3 us
  Pallas kernels  31.9 us (92%)
  between operations  1.29 us (4%)
  local copies, waits for them, and re-layouts  1.11 us (3%)
    pallas_call x1, Pallas kernels, on_device(): pl.pallas_call(functools.partial(kernel, nr, nc, width, rhs), out_shape=(...  31.9 us
    unnamed x2, local copies, waits for them, and re-layouts  1.11 us

profile of v6, /device:TPU:0, one launch (start us, length us, event | category | flops | bytes accessed | tf_op | source)
XLA Modules:
  0.0 34.3 jit_solution(15128175240170672300)
XLA Ops:
  1.3 31.9 %shard_map.68 = (f32[24,120]{1,0:T(8,128)S(1)}, f32[1,24]{1,0:T(1,128)S(1)}) custom-call(f32[1]{0:T(128)S(6)} %copy.9.azimuth_in, f32[3,120]{1,0:T(4,128)} %vertices_in.1, s32[4,120]{1,0:T(4,128)} %connect_in.1, s32[1,120]{1,0:T(1,128)} %bitcast.3, f32[24,120]{1,0:T(8,128)} %rhs_in.1), custom_call_target="tpu_custom_call" | custom-call | flops 100663296 | bytes 34560 | tf_op jit(solution)/shard_map/pallas_call | solution.py:349
  33.2 0.6 %copy.10 = f32[24,120]{1,0:T(8,128)} copy(f32[24,120]{1,0:T(8,128)S(1)} %get-tuple-element.8) | data formatting | bytes 23040
  33.8 0.5 %copy.11 = f32[24]{0:T(128)} copy(f32[24]{0:T(128)S(1)} %bitcast.2) | data formatting | bytes 192
